TPU v7x, 32 devices: a whole 2x2x4 slice. The times are simulated.
32 devices in a mesh: dp: 8 (over z, y), sp: 4 (over x, core).
Axes of the slice: x: 2, y: 2, z: 4, core: 2. Of those that a mesh axis runs over, the one named last changes fastest.
Arguments:
- tokens: bfloat16 [8, 1024, 1024], P('dp', 'sp'), may hold values from -6 to 6
- cotangent: bfloat16 [8, 1024, 1024], P('dp', 'sp'), may hold values from -6 to 6
- w_qkv: bfloat16 [2, 3, 1024, 1024], P(None, None, ('dp', 'sp')), may hold values from -0.1875 to 0.1875
- w_out: bfloat16 [2, 1024, 1024], P(None, ('dp', 'sp')), may hold values from -0.75 to 0.75
- w_up: bfloat16 [2, 1024, 4096], P(None, ('dp', 'sp')), may hold values from -0.1875 to 0.1875
- w_down: bfloat16 [2, 4096, 1024], P(None, ('dp', 'sp')), may hold values from -0.125 to 0.125
- gains: bfloat16 [2, 2, 1024], P(None, None, ('dp', 'sp')), may hold values from 0.5 to 1.5
- piece_order: int32 [8, 4], P('dp'), may hold values from 0 to 3, each once within a row
- doc_lengths: int32 [8, 4], P('dp'), may hold values from 1 to 512, 1024 in all within a row
Outputs:
- output: bfloat16 [8, 1024, 1024], P('dp', 'sp')
- input_grad: float32 [8, 1024, 1024], P('dp', 'sp')
- grad_qkv: float32 [2, 3, 1024, 1024], P(None, None, ('dp', 'sp'))
- grad_out: float32 [2, 1024, 1024], P(None, ('dp', 'sp'))
- grad_up: float32 [2, 1024, 4096], P(None, ('dp', 'sp'))
- grad_down: float32 [2, 4096, 1024], P(None, ('dp', 'sp'))
- grad_gains: float32 [2, 2, 1024], P(None, None, ('dp', 'sp'))
Inputs may be any that keep to these rules, and one draw needn't show every extreme that they name: Each row of piece_order names every index of sp once. `doc_lengths`: each row's lengths sum to 1024, and the longest is exactly 512.
All inputs are finite; a program needn't handle non-finite values.
Results may differ from a plain program's by a relative error of at most 0.019.
Values may be sent and summed in bfloat16 or wider, within the bound.
A program may use at most 320 MiB of HBM per device.

v0:
```python
import jax
import jax.numpy as jnp
from jax import lax
from jax.sharding import PartitionSpec as P

HEADS = 8
HD = 128


EPS = 1e-05
MASKED = -1e30


def normed(stream, gain):
    center = stream - jnp.mean(stream, axis=-1, keepdims=True)
    spread = jnp.mean(center * center, axis=-1, keepdims=True)
    return center * lax.rsqrt(spread + EPS) * gain.astype(jnp.float32)


def smooth_gate(value):
    return jax.nn.gelu(value, approximate=False)


def biased_scores(query, keys, query_pos, query_doc, key_pos, key_doc, slopes):
    product = jnp.einsum("rqhe,rkhe->rhqk", query, keys, preferred_element_type=jnp.float32)
    distance = (query_pos[:, :, None] - key_pos[:, None, :]).astype(jnp.float32)
    scores = product * HD ** (-0.5) + -slopes[None, :, None, None] * distance[:, None, :, :]
    allowed = (key_pos[:, None, :] <= query_pos[:, :, None]) & (
        key_doc[:, None, :] == query_doc[:, :, None]
    )
    return (scores, allowed[:, None, :, :])


def attend(query, keys, values, positions, documents, slopes):
    row_count, length, head_count, head_size = query.shape
    block = min(512, length)
    block_starts = jnp.arange(length // block, dtype=jnp.int32) * block

    def one_block(first_row):
        block_query = lax.dynamic_slice_in_dim(query, first_row, block, 1)
        block_pos = lax.dynamic_slice_in_dim(positions, first_row, block, 1)
        block_doc = lax.dynamic_slice_in_dim(documents, first_row, block, 1)
        scores, allowed = biased_scores(
            block_query, keys, block_pos, block_doc, positions, documents, slopes
        )
        masked = jnp.where(allowed, scores, MASKED)
        top_score = jnp.max(masked, axis=-1, keepdims=True)
        expo = jnp.where(allowed, jnp.exp(masked - top_score), 0.0)
        total = jnp.sum(expo, axis=-1, keepdims=True)
        probs_low = (expo / total).astype(jnp.bfloat16)
        result = jnp.einsum(
            "rhqk,rkhe->rqhe", probs_low, values, preferred_element_type=jnp.float32
        )
        return (result.astype(jnp.bfloat16), (top_score + jnp.log(total))[..., 0])

    results, log_sums = lax.map(one_block, block_starts)
    results = jnp.moveaxis(results, 0, 1).reshape(row_count, length, head_count, head_size)
    log_sums = jnp.moveaxis(log_sums, 0, 2).reshape(row_count, head_count, length)
    return (results, log_sums)


def attend_back(query, keys, values, grad_heads, log_sums, positions, documents, slopes):
    row_count, length, head_count, head_size = query.shape
    block = min(512, length)
    block_starts = jnp.arange(length // block, dtype=jnp.int32) * block

    def one_block(carry, first_row):
        d_keys, d_values = carry
        block_query = lax.dynamic_slice_in_dim(query, first_row, block, 1)
        block_grad = lax.dynamic_slice_in_dim(grad_heads, first_row, block, 1)
        block_pos = lax.dynamic_slice_in_dim(positions, first_row, block, 1)
        block_doc = lax.dynamic_slice_in_dim(documents, first_row, block, 1)
        block_lse = lax.dynamic_slice_in_dim(log_sums, first_row, block, 2)
        scores, allowed = biased_scores(
            block_query, keys, block_pos, block_doc, positions, documents, slopes
        )
        probs = jnp.where(allowed, jnp.exp(scores - block_lse[..., None]), 0.0)
        probs_low = probs.astype(jnp.bfloat16)
        d_values = d_values + jnp.einsum(
            "rhqk,rqhe->rkhe", probs_low, block_grad, preferred_element_type=jnp.float32
        )
        d_probs = jnp.einsum(
            "rqhe,rkhe->rhqk", block_grad, values, preferred_element_type=jnp.float32
        )
        inner = jnp.sum(probs * d_probs, axis=-1, keepdims=True)
        d_scores = (probs * (d_probs - inner)).astype(jnp.bfloat16)
        d_query = jnp.einsum(
            "rhqk,rkhe->rqhe", d_scores, keys, preferred_element_type=jnp.float32
        ) * HD ** (-0.5)
        d_keys = d_keys + jnp.einsum(
            "rhqk,rqhe->rkhe", d_scores, block_query, preferred_element_type=jnp.float32
        ) * HD ** (-0.5)
        return ((d_keys, d_values), d_query.astype(jnp.bfloat16))

    zeros = jnp.zeros(keys.shape, jnp.float32)
    (d_keys, d_values), d_queries = lax.scan(one_block, (zeros, zeros), block_starts)
    d_queries = jnp.moveaxis(d_queries, 0, 1).reshape(row_count, length, head_count, head_size)
    return (d_queries, d_keys.astype(jnp.bfloat16), d_values.astype(jnp.bfloat16))


def layer_forward(stream, weights, context):
    w_qkv, w_out, w_up, w_down, gains = weights
    positions, documents, slopes, row_count, local_len = context
    normed_in = normed(stream, gains[0]).astype(jnp.bfloat16)
    projected = jnp.einsum(
        "td,jde->jte", normed_in, w_qkv, preferred_element_type=jnp.float32
    ).astype(jnp.bfloat16)
    projected = projected.reshape(3, row_count, local_len, HEADS, HD)
    heads = lax.all_to_all(projected, "sp", split_axis=3, concat_axis=2, tiled=True)
    attended, log_sums = attend(heads[0], heads[1], heads[2], positions, documents, slopes)
    attended = lax.all_to_all(attended, "sp", split_axis=1, concat_axis=2, tiled=True)
    attended = attended.reshape(row_count * local_len, HEADS * HD)
    mid = stream + jnp.dot(attended, w_out, preferred_element_type=jnp.float32)
    normed_mid = normed(mid, gains[1]).astype(jnp.bfloat16)
    pre = jnp.dot(normed_mid, w_up, preferred_element_type=jnp.float32)
    hidden = smooth_gate(pre).astype(jnp.bfloat16)
    result = mid + jnp.dot(hidden, w_down, preferred_element_type=jnp.float32)
    return (result, (stream, normed_in, heads, log_sums, attended, mid, normed_mid, pre, hidden))


def layer_backward(grad, saved, weights, context):
    w_qkv, w_out, w_up, w_down, gains = weights
    positions, documents, slopes, row_count, local_len = context
    stream, normed_in, heads, log_sums, attended, mid, normed_mid, pre, hidden = saved
    grad_low = grad.astype(jnp.bfloat16)
    d_down = jnp.dot(hidden.T, grad_low, preferred_element_type=jnp.float32)
    d_hidden = jnp.dot(grad_low, w_down.T, preferred_element_type=jnp.float32)
    unused_gate, pull_gate = jax.vjp(smooth_gate, pre)
    d_pre = pull_gate(d_hidden)[0].astype(jnp.bfloat16)
    d_up = jnp.dot(normed_mid.T, d_pre, preferred_element_type=jnp.float32)
    d_normed = jnp.dot(d_pre, w_up.T, preferred_element_type=jnp.float32)
    unused_mid, pull_mid = jax.vjp(normed, mid, gains[1].astype(jnp.float32))
    d_mid_norm, d_gain_mid = pull_mid(d_normed)
    d_mid = grad + d_mid_norm
    mid_low = d_mid.astype(jnp.bfloat16)
    d_out = jnp.dot(attended.T, mid_low, preferred_element_type=jnp.float32)
    d_attended = jnp.dot(mid_low, w_out.T, preferred_element_type=jnp.float32).astype(jnp.bfloat16)
    d_attended = d_attended.reshape(row_count, local_len, HEADS, HD)
    grad_heads = lax.all_to_all(d_attended, "sp", split_axis=2, concat_axis=1, tiled=True)
    d_query, d_keys, d_values = attend_back(
        heads[0], heads[1], heads[2], grad_heads, log_sums, positions, documents, slopes
    )
    d_projected = lax.all_to_all(
        jnp.stack([d_query, d_keys, d_values]), "sp", split_axis=2, concat_axis=3, tiled=True
    )
    d_projected = d_projected.reshape(3, row_count * local_len, HEADS * HD)
    d_qkv = jnp.einsum("td,jte->jde", normed_in, d_projected, preferred_element_type=jnp.float32)
    d_in = jnp.einsum("jte,jde->td", d_projected, w_qkv, preferred_element_type=jnp.float32)
    unused_in, pull_in = jax.vjp(normed, stream, gains[0].astype(jnp.float32))
    d_stream_norm, d_gain_in = pull_in(d_in)
    grad_next = d_mid + d_stream_norm
    return (grad_next, (d_qkv, d_out, d_up, d_down, jnp.stack([d_gain_in, d_gain_mid])))


def shards(tokens, cotangent, w_qkv, w_out, w_up, w_down, gains, piece_order, doc_lengths):
    row_count, local_len, width = tokens.shape
    sp_count = lax.axis_size("sp")
    sp_rank = lax.axis_index("sp")
    length = local_len * sp_count
    heads_dev = HEADS // sp_count
    layer_count = w_qkv.shape[0]
    offsets = jnp.arange(local_len, dtype=jnp.int32)
    positions = (piece_order[:, :, None] * local_len + offsets[None, None, :]).reshape(
        row_count, length
    )
    bounds = jnp.cumsum(doc_lengths, axis=1)
    documents = jnp.sum((positions[:, :, None] >= bounds[:, None, :]).astype(jnp.int32), axis=2)
    head_ids = (sp_rank * heads_dev + jnp.arange(heads_dev, dtype=jnp.int32)).astype(jnp.float32)
    slopes = jnp.exp2(-8.0 * (head_ids + 1.0) / HEADS)
    context = (positions, documents, slopes, row_count, local_len)

    def fetch(layer_id):
        return (
            lax.all_gather(w_qkv[layer_id], ("dp", "sp"), axis=1, tiled=True),
            lax.all_gather(w_out[layer_id], ("dp", "sp"), axis=0, tiled=True),
            lax.all_gather(w_up[layer_id], ("dp", "sp"), axis=0, tiled=True),
            lax.all_gather(w_down[layer_id], ("dp", "sp"), axis=0, tiled=True),
            lax.all_gather(gains[layer_id], ("dp", "sp"), axis=1, tiled=True),
        )

    stream = tokens.reshape(row_count * local_len, width).astype(jnp.float32)
    layer_inputs = []
    for layer_id in range(layer_count):
        weights = fetch(layer_id)
        layer_inputs.append(stream)
        stream, saved = layer_forward(stream, weights, context)
    output = stream.astype(jnp.bfloat16).reshape(row_count, local_len, width)
    grad = cotangent.reshape(row_count * local_len, width).astype(jnp.float32)
    grad_layers = [None] * layer_count
    for layer_id in reversed(range(layer_count)):
        weights = fetch(layer_id)
        unused_out, saved = layer_forward(layer_inputs[layer_id], weights, context)
        grad, terms = layer_backward(grad, saved, weights, context)
        grad_layers[layer_id] = (
            lax.psum_scatter(terms[0], ("dp", "sp"), scatter_dimension=1, tiled=True),
            lax.psum_scatter(terms[1], ("dp", "sp"), scatter_dimension=0, tiled=True),
            lax.psum_scatter(terms[2], ("dp", "sp"), scatter_dimension=0, tiled=True),
            lax.psum_scatter(terms[3], ("dp", "sp"), scatter_dimension=0, tiled=True),
            lax.psum_scatter(terms[4], ("dp", "sp"), scatter_dimension=1, tiled=True),
        )
    grad_qkv = jnp.stack([entry[0] for entry in grad_layers])
    grad_out = jnp.stack([entry[1] for entry in grad_layers])
    grad_up = jnp.stack([entry[2] for entry in grad_layers])
    grad_down = jnp.stack([entry[3] for entry in grad_layers])
    grad_gains = jnp.stack([entry[4] for entry in grad_layers])
    input_grad = grad.reshape(row_count, local_len, width)
    return (output, input_grad, grad_qkv, grad_out, grad_up, grad_down, grad_gains)


def solution(mesh):
    return jax.shard_map(
        shards,
        mesh=mesh,
        in_specs=(
            P("dp", "sp", None),
            P("dp", "sp", None),
            P(None, None, ("dp", "sp"), None),
            P(None, ("dp", "sp"), None),
            P(None, ("dp", "sp"), None),
            P(None, ("dp", "sp"), None),
            P(None, None, ("dp", "sp")),
            P("dp", None),
            P("dp", None),
        ),
        out_specs=(
            P("dp", "sp", None),
            P("dp", "sp", None),
            P(None, None, ("dp", "sp"), None),
            P(None, ("dp", "sp"), None),
            P(None, ("dp", "sp"), None),
            P(None, ("dp", "sp"), None),
            P(None, None, ("dp", "sp")),
        ),
        check_vma=False,
    )
```

profile of v0, /device:TPU:14, one launch (start us, length us, event | category | flops | bytes accessed | tf_op | source)
XLA Modules:
  0.0 2577.5 jit_solution(17470003736623699895)
XLA Ops:
  16.6 31.0 %all-gather = bf16[1,2,1024]{1,0,2:T(2,128)(2,1)S(1)} all-gather(bf16[1,2,32]{1,0,2:T(2,128)(2,1)S(1)} %copy.220), channel_id=2, replica_groups=mesh['dp'=8,'sp'=4] {'dp','sp'}, dimensions={2}, use_global_device_ids=true | all-gather | bytes 4224 | tf_op jit(solution)/shard_map/all_gather | solution.py:178
  48.6 6.3 fusion.406
  54.9 27.6 %all-gather.19.cloned.1.call-done = bf16[1,3,1024,1024]{3,2,1,0:T(8,128)(2,1)} async-done(((bf16[1,3,32,1024]{3,2,1,0:T(8,128)(2,1)}), bf16[1,3,1024,1024]{3,2,1,0:T(8,128)(2,1)}) %all-gather.19.cloned.1.call-update) | async-done | bytes 6291472 | tf_op jit(solution)/shard_map/all_gather | solution.py:174
  94.9 19.8 all-to-all-done
  116.7 27.0 %while.90 = (s32[]{:T(128)}, bf16[2,1,512,2,128]{4,2,0,3,1:T(8,128)(2,1)}, s32[2]{0:T(128)S(1)}, s32[1,1024]{1,0:T(1,128)S(1)}, s32[1,1024]{1,0:T(1,128)S(1)}, /...) while((s32[]{:T(128)}, ...), condition=%wide.region_7.8_spmd.clone, body=%wide.region_4.7_spmd.clone.sunk | while | flops 549062656 | bytes 15776475 | solution.py:56
  151.7 34.8 %all-gather.5 = bf16[1,2,1024]{1,0,2:T(2,128)(2,1)S(1)} all-gather(bf16[1,2,32]{1,0,2:T(2,128)(2,1)S(1)} %copy.221), channel_id=7, replica_groups=mesh['dp'=8,'sp'=4] {'dp','sp'}, dimensions={2}, use_global_device_ids=true | all-gather | bytes 4224 | tf_op jit(solution)/shard_map/all_gather | solution.py:178
  186.5 6.3 fusion.404
  195.8 28.2 %all-gather.23.cloned.1.call-done = bf16[1,1024,4096]{2,1,0:T(8,128)(2,1)} async-done(((bf16[1,32,4096]{2,1,0:T(8,128)(2,1)}), bf16[1,1024,4096]{2,1,0:T(8,128)(2,1)}) %all-gather.23.cloned.1.call-update) | async-done | bytes 8388624 | tf_op jit(solution)/shard_map/all_gather | solution.py:176
  224.0 79.4 %all-gather.25.cloned.1.call-done = bf16[1,4096,1024]{2,1,0:T(8,128)(2,1)} async-done(((bf16[1,128,1024]{2,1,0:T(8,128)(2,1)}), bf16[1,4096,1024]{2,1,0:T(8,128)(2,1)}) %all-gather.25.cloned.1.call-update) | async-done | bytes 8388624 | tf_op jit(solution)/shard_map/all_gather | solution.py:177
  303.4 19.4 fusion.527
  323.1 51.2 %all-gather.27.cloned.1.call-done = bf16[1,3,1024,1024]{3,2,1,0:T(8,128)(2,1)} async-done(((bf16[1,3,32,1024]{3,2,1,0:T(8,128)(2,1)}), bf16[1,3,1024,1024]{3,2,1,0:T(8,128)(2,1)}) %all-gather.27.cloned.1.call-update) | async-done | bytes 6291472 | tf_op jit(solution)/shard_map/all_gather | solution.py:174
  380.9 6.0 all-to-all-start.2
  386.9 20.3 all-to-all-done.2
  410.5 20.0 while.92
  439.6 20.0 while.93
  474.5 42.3 %all-gather.31.cloned.1.call-done = bf16[1,1024,4096]{2,1,0:T(8,128)(2,1)} async-done(((bf16[1,32,4096]{2,1,0:T(8,128)(2,1)}), bf16[1,1024,4096]{2,1,0:T(8,128)(2,1)}) %all-gather.31.cloned.1.call-update) | async-done | bytes 8388624 | tf_op jit(solution)/shard_map/all_gather | solution.py:176
  516.8 8.2 fusion.180
  525.0 71.3 %all-gather.33.cloned.1.call-done = bf16[1,4096,1024]{2,1,0:T(8,128)(2,1)} async-done(((bf16[1,128,1024]{2,1,0:T(8,128)(2,1)}), bf16[1,4096,1024]{2,1,0:T(8,128)(2,1)}) %all-gather.33.cloned.1.call-update) | async-done | bytes 8388624 | tf_op jit(solution)/shard_map/all_gather | solution.py:177
  596.3 14.7 add_convert_fusion.1
  618.0 6.0 all-to-all-start.5
  634.3 22.1 while.94
  663.0 5.8 all-to-all-start.6
  669.2 7.8 fusion.190
  677.0 10.4 all-to-all-done.6
  702.5 15.0 add_convert_fusion
  729.5 7.3 all-to-all-done.8
  739.6 22.0 while.95
  773.0 17.5 all-to-all-done.9
  812.5 6.6 convolution_bitcast_fusion
  819.0 18.6 copy.195
  837.6 6.6 convolution_bitcast_fusion.1
  844.2 18.5 copy.193
  863.7 16.0 fusion.241
  881.0 16.0 fusion.240
  898.9 8.3 fusion.502
  909.1 8.2 fusion.503
  918.7 27.1 %while.91 = (s32[]{:T(128)}, bf16[2,1,512,2,128]{4,2,0,3,1:T(8,128)(2,1)}, s32[2]{0:T(128)S(1)}, s32[1,1024]{1,0:T(1,128)S(1)}, s32[1,1024]{1,0:T(1,128)S(1)}, /...) while((s32[]{:T(128)}, ...), condition=%wide.region_15.16_spmd.clone, body=%wide.region_12.15_spmd.clone.sunk | while | flops 549062656 | bytes 15776475 | solution.py:56
  948.3 6.0 all-to-all-start.3
  954.3 7.4 all-to-all-done.3
  968.5 20.2 fusion.382
  991.0 16.6 reduce-scatter.25.cloned.1.call-done
  1008.9 137.9 %reduce-scatter.15.cloned.1.call-done = f32[32,1024]{1,0:T(8,128)} async-done(((f32[1024,1024]{1,0:T(8,128)}), f32[32,1024]{1,0:T(8,128)}) %reduce-scatter.15.cloned.1.call-update) | async-done | bytes 131088 | tf_op jit(solution)/shard_map/reduce_scatter | solution.py:196
  1146.8 138.9 %reduce-scatter.13.cloned.1.call-done = f32[32,1024]{1,0:T(8,128)} async-done(((f32[1024,1024]{1,0:T(8,128)}), f32[32,1024]{1,0:T(8,128)}) %reduce-scatter.13.cloned.1.call-update) | async-done | bytes 131088 | tf_op jit(solution)/shard_map/reduce_scatter | solution.py:196
  1287.4 533.4 %all-reduce.5.cloned.1.call-done = (f32[3,1024,1024]{2,0,1:T(4,128)}, f32[3,1024,1024]{2,0,1:T(4,128)}) async-done(((f32[3,1024,1024]{2,0,1:T(4,128)}, f32[3,1024,1024]{2,0,1:T(4,128)}), (f32[3,1024,1024]{2,0,1:T(4,128)}, f32[3,1024,1024]{2,0,1:T(4,128)})) %all-reduce.5.cloned.1.call-update) | async-done | bytes 25165840
  1823.6 184.4 %reduce-scatter.23.cloned.1.call-done = f32[128,1024]{1,0:T(8,128)} async-done(((f32[4096,1024]{1,0:T(8,128)}), f32[128,1024]{1,0:T(8,128)}) %reduce-scatter.23.cloned.1.call-update) | async-done | bytes 524304 | tf_op jit(solution)/shard_map/reduce_scatter | solution.py:198
  2008.0 186.8 %reduce-scatter.21.cloned.1.call-done = f32[128,1024]{1,0:T(8,128)} async-done(((f32[4096,1024]{1,0:T(8,128)}), f32[128,1024]{1,0:T(8,128)}) %reduce-scatter.21.cloned.1.call-update) | async-done | bytes 524304 | tf_op jit(solution)/shard_map/reduce_scatter | solution.py:198
  2197.0 184.5 %reduce-scatter.19.cloned.1.call-done = f32[32,4096]{1,0:T(8,128)} async-done(((f32[1024,4096]{1,0:T(8,128)}), f32[32,4096]{1,0:T(8,128)}) %reduce-scatter.19.cloned.1.call-update) | async-done | bytes 524304 | tf_op jit(solution)/shard_map/reduce_scatter | solution.py:197
  2381.5 186.8 %reduce-scatter.17.cloned.1.call-done = f32[32,4096]{1,0:T(8,128)} async-done(((f32[1024,4096]{1,0:T(8,128)}), f32[32,4096]{1,0:T(8,128)}) %reduce-scatter.17.cloned.1.call-update) | async-done | bytes 524304 | tf_op jit(solution)/shard_map/reduce_scatter | solution.py:197
  (557 shorter events, 300.3 us)
Async XLA Ops:
  7.2 40.4 %copy-start.12 = (bf16[1,256,1024]{2,1,0:T(8,128)(2,1)S(1)}, bf16[1,256,1024]{2,1,0:T(8,128)(2,1)}, u32[]{:S(2)}) copy-start(bf16[1,256,1024]{2,1,0:T(8,128)(2,1)} %param.21) | copy-start | bytes 1572868
  7.2 75.3 %all-gather.19.cloned.1.call-start = ((), (), s32[]{:S(2)}) async-start(), calls=%async_computation.24 | async-start | bytes 6488064 | tf_op jit(solution)/shard_map/all_gather | solution.py:174
  9.1 184.0 %all-gather.21.cloned.1.call-start = ((), (), s32[]{:S(2)}) async-start(), calls=%async_computation.25 | async-start | bytes 2162688 | tf_op jit(solution)/shard_map/all_gather | solution.py:175
  10.7 213.3 %all-gather.23.cloned.1.call-start = ((), (), s32[]{:S(2)}) async-start(), calls=%async_computation.26 | async-start | bytes 8650752 | tf_op jit(solution)/shard_map/all_gather | solution.py:176
  12.6 290.8 %all-gather.25.cloned.1.call-start = ((), (), s32[]{:S(2)}) async-start(), calls=%async_computation.27 | async-start | bytes 8650752 | tf_op jit(solution)/shard_map/all_gather | solution.py:177
  14.6 359.7 %all-gather.27.cloned.1.call-start = ((), (), s32[]{:S(2)}) async-start(), calls=%async_computation.28 | async-start | bytes 6488064 | tf_op jit(solution)/shard_map/all_gather | solution.py:174
  15.2 455.5 %all-gather.29.cloned.1.call-start = ((), (), s32[]{:S(2)}) async-start(), calls=%async_computation.29 | async-start | bytes 2162688 | tf_op jit(solution)/shard_map/all_gather | solution.py:175
  15.7 501.0 %all-gather.31.cloned.1.call-start = ((), (), s32[]{:S(2)}) async-start(), calls=%async_computation.30 | async-start | bytes 8650752 | tf_op jit(solution)/shard_map/all_gather | solution.py:176
  47.7 39.5 %copy-start.77 = (f32[256]{0:T(256)}, f32[256]{0:T(256)S(1)}, u32[]{:S(2)}) copy-start(f32[256]{0:T(256)S(1)} %broadcast_multiply_fusion.5) | copy-start | bytes 3076
  48.6 38.6 %copy-start.84 = (f32[256]{0:T(256)}, f32[256]{0:T(256)S(1)}, u32[]{:S(2)}) copy-start(f32[256]{0:T(256)S(1)} %fusion.433) | copy-start | bytes 3076
  54.9 32.3 %copy-start.68 = (f32[1024]{0:T(1024)}, f32[1024]{0:T(1024)S(1)}, u32[]{:S(2)}) copy-start(f32[1024]{0:T(1024)S(1)} %get-tuple-element.1062) | copy-start | bytes 12292
  54.9 248.5 %copy-start.61 = (f32[1024]{0:T(1024)}, f32[1024]{0:T(1024)S(1)}, u32[]{:S(2)}) copy-start(f32[1024]{0:T(1024)S(1)} %get-tuple-element.1061) | copy-start | bytes 12292
  89.2 25.5 all-to-all-start
  143.7 49.4 %copy-start.13 = (bf16[1,256,1024]{2,1,0:T(8,128)(2,1)S(1)}, bf16[1,256,1024]{2,1,0:T(8,128)(2,1)}, u32[]{:S(2)}) copy-start(bf16[1,256,1024]{2,1,0:T(8,128)(2,1)} %param.21) | copy-start | bytes 1572868
  146.1 46.6 %all-to-all-start.1 = ((bf16[1,1024,2,128]{3,2,0,1:T(2,128)(2,1)}), bf16[1,1024,2,128]{3,2,0,1:T(2,128)(2,1)S(1)}, u32[]{:S(2)}, u32[]{:S(2)}) async-start(bf16[1,1024,2,128]{3,2,0,1:T(2,128)(2,1)} %copy.158), calls=%async_computation.1 | async-start | bytes 1048576 | tf_op jit(solution)/shard_map/all_to_all | solution.py:111
  150.9 445.4 %all-gather.33.cloned.1.call-start = ((), (), s32[]{:S(2)}) async-start(), calls=%async_computation.31 | async-start | bytes 8650752 | tf_op jit(solution)/shard_map/all_gather | solution.py:177
  192.8 181.5 %copy-start.71 = (f32[1024]{0:T(1024)}, f32[1024]{0:T(1024)S(1)}, u32[]{:S(2)}) copy-start(f32[1024]{0:T(1024)S(1)} %get-tuple-element.1060) | copy-start | bytes 12292
  195.5 107.9 %copy-start.42 = (f32[256,1024]{1,0:T(8,128)}, f32[256,1024]{1,0:T(8,128)S(1)}, u32[]{:S(2)}) copy-start(f32[256,1024]{1,0:T(8,128)S(1)} %get-tuple-element.1254) | copy-start | bytes 3145732
  322.8 147.8 %copy-start.8 = (f32[256,1024]{1,0:T(8,128)}, f32[256,1024]{1,0:T(8,128)S(1)}, u32[]{:S(2)}) copy-start(f32[256,1024]{1,0:T(8,128)S(1)} %get-tuple-element.1256) | copy-start | bytes 3145732
  322.8 56.1 %copy-start.87 = (f32[256]{0:T(256)}, f32[256]{0:T(256)S(1)}, u32[]{:S(2)}) copy-start(f32[256]{0:T(256)S(1)} %broadcast_multiply_fusion.3) | copy-start | bytes 3076
  323.1 55.9 %copy-start.95 = (f32[256]{0:T(256)}, f32[256]{0:T(256)S(1)}, u32[]{:S(2)}) copy-start(f32[256]{0:T(256)S(1)} %multiply_reduce_fusion.11) | copy-start | bytes 3076
  323.1 55.9 %copy-start.91 = (f32[256]{0:T(256)}, f32[256]{0:T(256)S(1)}, u32[]{:S(2)}) copy-start(f32[256]{0:T(256)S(1)} %fusion.434) | copy-start | bytes 3076
  380.9 26.3 %all-to-all-start.2 = ((bf16[3,1,256,8,128]{4,2,0,1,3:T(8,128)(2,1)}), bf16[3,1,256,8,128]{4,2,0,1,3:T(8,128)(2,1)}, u32[]{:S(2)}, u32[]{:S(2)}) async-start(bf16[3,1,256,8,128]{4,2,0,1,3:T(8,128)(2,1)} %copy.162), calls=%async_computation.2 | async-start | bytes 3145728 | tf_op jit(solution)/shard_map/all_to_all | solution.py:109
  432.9 29.4 %all-to-all-start.4 = ((bf16[1,1024,2,128]{3,2,0,1:T(2,128)(2,1)}), bf16[1,1024,2,128]{3,2,0,1:T(2,128)(2,1)}, u32[]{:S(2)}, u32[]{:S(2)}) async-start(bf16[1,1024,2,128]{3,2,0,1:T(2,128)(2,1)} %copy.171), calls=%async_computation.4 | async-start | bytes 1048576 | tf_op jit(solution)/shard_map/all_to_all | solution.py:111
  462.3 155.7 %all-to-all-start.7 = ((bf16[1,1024,2,128]{3,2,0,1:T(2,128)(2,1)}), bf16[1,1024,2,128]{3,2,0,1:T(2,128)(2,1)}, u32[]{:S(2)}, u32[]{:S(2)}) async-start(bf16[1,1024,2,128]{3,2,0,1:T(2,128)(2,1)} %copy.182), calls=%async_computation.7 | async-start | bytes 1048576 | tf_op jit(solution)/shard_map/all_to_all | solution.py:111
  466.7 50.1 %copy-start.64 = (f32[1024]{0:T(1024)S(1)}, f32[1024]{0:T(1024)}, u32[]{:S(2)}) copy-start(f32[1024]{0:T(1024)} %get-tuple-element.1059) | copy-start | bytes 12292
  473.3 140.9 %copy-start.73 = (f32[256]{0:T(256)}, f32[256]{0:T(256)S(1)}, u32[]{:S(2)}) copy-start(f32[256]{0:T(256)S(1)} %broadcast_multiply_fusion.1) | copy-start | bytes 3076
  474.5 139.7 %copy-start.80 = (f32[256]{0:T(256)}, f32[256]{0:T(256)S(1)}, u32[]{:S(2)}) copy-start(f32[256]{0:T(256)S(1)} %fusion.435) | copy-start | bytes 3076
  516.8 79.5 %copy-start.48 = (bf16[1,256,1024]{2,1,0:T(8,128)(2,1)S(1)}, bf16[1,256,1024]{2,1,0:T(8,128)(2,1)}, u32[]{:S(2)}) copy-start(bf16[1,256,1024]{2,1,0:T(8,128)(2,1)} %param.22) | copy-start | bytes 1572868
  525.0 86.0 %copy-start.22 = (f32[256,1024]{1,0:T(8,128)S(1)}, f32[256,1024]{1,0:T(8,128)}, u32[]{:S(2)}) copy-start(f32[256,1024]{1,0:T(8,128)} %copy-done.21) | copy-start | bytes 3145732
  618.0 13.6 all-to-all-start.5
  663.0 24.3 all-to-all-start.6
  668.9 51.3 %copy-start.75 = (f32[256]{0:T(256)}, f32[256]{0:T(256)S(1)}, u32[]{:S(2)}) copy-start(f32[256]{0:T(256)S(1)} %broadcast_multiply_fusion) | copy-start | bytes 3076
  669.2 51.0 %copy-start.82 = (f32[256]{0:T(256)}, f32[256]{0:T(256)S(1)}, u32[]{:S(2)}) copy-start(f32[256]{0:T(256)S(1)} %fusion.436) | copy-start | bytes 3076
  723.7 13.1 all-to-all-start.8
  766.2 24.3 all-to-all-start.9
  771.4 24.2 copy-start.69
  771.4 24.2 copy-start.78
  771.4 217.3 %reduce-scatter.27.cloned.1.call-start = ((), (), s32[]{:S(2)}) async-start(), calls=%async_computation.33 | async-start | bytes 540672
  772.9 234.6 %reduce-scatter.25.cloned.1.call-start = ((), (), s32[]{:S(2)}) async-start(), calls=%async_computation.32 | async-start | bytes 540672
  804.2 342.7 %reduce-scatter.15.cloned.1.call-start = ((), (), s32[]{:S(2)}) async-start(), calls=%async_computation.19 | async-start | bytes 4325376 | tf_op jit(solution)/shard_map/reduce_scatter | solution.py:196
  807.0 478.8 %reduce-scatter.13.cloned.1.call-start = ((), (), s32[]{:S(2)}) async-start(), calls=%async_computation.18 | async-start | bytes 4325376 | tf_op jit(solution)/shard_map/reduce_scatter | solution.py:196
  811.1 1009.7 %all-reduce.5.cloned.1.call-start = ((), (), s32[]{:S(2)}) async-start(), calls=%async_computation.34 | async-start | bytes 67108864
  862.7 1145.3 %reduce-scatter.23.cloned.1.call-start = ((), (), s32[]{:S(2)}) async-start(), calls=%async_computation.23 | async-start | bytes 17301504 | tf_op jit(solution)/shard_map/reduce_scatter | solution.py:198
  879.8 1315.0 %reduce-scatter.21.cloned.1.call-start = ((), (), s32[]{:S(2)}) async-start(), calls=%async_computation.22 | async-start | bytes 17301504 | tf_op jit(solution)/shard_map/reduce_scatter | solution.py:198
  897.0 1484.5 %reduce-scatter.19.cloned.1.call-start = ((), (), s32[]{:S(2)}) async-start(), calls=%async_computation.21 | async-start | bytes 17301504 | tf_op jit(solution)/shard_map/reduce_scatter | solution.py:197
  907.2 1661.0 %reduce-scatter.17.cloned.1.call-start = ((), (), s32[]{:S(2)}) async-start(), calls=%async_computation.20 | async-start | bytes 17301504 | tf_op jit(solution)/shard_map/reduce_scatter | solution.py:197
  948.3 13.3 all-to-all-start.3
  (97 other events, 677.0 us)
Sparse Core Ops, SparseCore 0:
  11.5 70.9 all-gather.18
  85.4 55.0 all-gather.20
  143.3 80.6 all-gather.22
  227.3 76.0 all-gather.24
  306.2 68.0 all-gather.26
  377.0 55.4 all-gather.28
  435.9 80.7 all-gather.30
  520.2 76.0 all-gather.32
  774.5 101.2 reduce-scatter.26
  878.0 129.5 reduce-scatter.24
  1009.8 136.9 reduce-scatter.14
  1149.0 136.7 reduce-scatter.12
  1292.2 528.5 all-reduce.4
  1823.0 184.8 reduce-scatter.22
  2010.2 184.4 reduce-scatter.20
  2197.0 184.4 reduce-scatter.18
  2383.7 184.4 reduce-scatter.16
where the time goes:
time: 2590 us; the launch traced here: 2580 us
  waiting for transfers between devices  1950 us (75%)
  matrix products  266 us (10%)
  local copies, waits for them, and re-layouts  143 us (6%)
  blocking collectives  65.7 us (3%)
  starting transfers between devices  56.3 us (2%)
  other arithmetic  51.8 us (2%)
    unnamed x20, waiting for transfers between devices  553 us
    reduce_scatter x2, waiting for transfers between devices, shards(): lax.psum_scatter(terms[2], ('dp', 'sp'), scatter_dimension=0, tiled=True)  371 us
    reduce_scatter x2, waiting for transfers between devices, shards(): lax.psum_scatter(terms[3], ('dp', 'sp'), scatter_dimension=0, tiled=True)  371 us
    reduce_scatter x2, waiting for transfers between devices, shards(): lax.psum_scatter(terms[1], ('dp', 'sp'), scatter_dimension=0, tiled=True)  277 us
    all_gather x2, waiting for transfers between devices, fetch(): lax.all_gather(w_down[layer_id], ('dp', 'sp'), axis=0, tiled=True)  151 us
    all_gather x2, waiting for transfers between devices, fetch(): lax.all_gather(w_qkv[layer_id], ('dp', 'sp'), axis=1, tiled=True)  78.8 us
    all_gather x2, waiting for transfers between devices, fetch(): lax.all_gather(w_up[layer_id], ('dp', 'sp'), axis=0, tiled=True)  70.5 us
    all_gather x2, blocking collectives, fetch(): lax.all_gather(gains[layer_id], ('dp', 'sp'), axis=1, tiled=True)  65.7 us
  transfers between devices with their start and end apart: 27, of which 20 were waited for; matrix products, arithmetic and copies ran while one was open for 14% of the time, Pallas kernels for 0%

commit v1 on v0

v1 whole, which is shorter than its diff:
```python
import functools

import jax
import jax.numpy as jnp
from jax import lax
from jax.experimental import pallas as pl
from jax.experimental.pallas import tpu as pltpu
from jax.sharding import PartitionSpec as P

HEADS = 8
HD = 128
EPS = 1e-05
MASKED = -1e30
MESH = pl.DeviceIdType.MESH
BF = jnp.bfloat16
F32 = jnp.float32
QKV, OUT, UP, DOWN = range(4)


def nn(a, b):
    return lax.dot_general(a, b, (((1,), (0,)), ((), ())), preferred_element_type=F32)


def nt(a, b):
    return lax.dot_general(a, b, (((1,), (1,)), ((), ())), preferred_element_type=F32)


def tn(a, b):
    return lax.dot_general(a, b, (((0,), (0,)), ((), ())), preferred_element_type=F32)


class Dims:
    def __init__(self, dp_n, sp_n, layers, tok, width, ff, docs):
        self.dp_n, self.sp_n, self.layers, self.tok, self.width = dp_n, sp_n, layers, tok, width
        self.z_n = 4 if dp_n % 4 == 0 else 1
        self.y_n = dp_n // self.z_n
        self.x_n = sp_n // 2
        self.rows = width // (dp_n * sp_n)
        self.heads = HEADS // sp_n
        self.dh = width // sp_n
        self.hid = ff // sp_n
        self.hid_own = ff // (dp_n * sp_n)
        self.docs = docs
        self.chunk = min(256, tok)
        self.n_width = width // self.chunk
        self.n_hid = self.hid // self.chunk
        self.back = self.x_n
        self.pairs = [(i, b) for i in range(sp_n) for b in range(max(0, i - self.back), i + 1)]

    def block_shape(self, which):
        return {
            QKV: (self.sp_n, self.rows, 3 * self.dh),
            OUT: (self.rows, self.width),
            UP: (self.sp_n, self.rows, self.hid),
            DOWN: (self.hid_own, self.width),
        }[which]


class Place:
    def __init__(self, d):
        self.d = d
        self.r = lax.axis_index("dp")
        self.s = lax.axis_index("sp")
        self.z, self.y = self.r // d.y_n, self.r % d.y_n
        self.x, self.c = self.s // 2, self.s % 2
        self.partner = self.x * 2 + (self.c + 1) % 2

    def slot(self, step):
        return ((self.x + step // 2) % self.d.x_n) * 2 + (self.c + step % 2) % 2

    def zpeer(self, dz):
        return (self.z + dz) % self.d.z_n

    def ypeer(self, dy):
        return (self.y + dy) % self.d.y_n

    def dev(self, z, y):
        return (z * self.d.y_n + y, self.s)

    def moved(self):
        d = self.d
        flat = self.r * d.sp_n + self.s
        goal = (flat % d.dp_n, flat // d.dp_n)
        mine = self.s * d.dp_n + self.r
        source = (mine // d.sp_n, mine % d.sp_n)
        stays = flat == mine
        return goal, source, stays

    def barrier(self):
        d = self.d
        sem = pltpu.get_barrier_semaphore()
        peers = [(self.r, self.slot(t)) for t in range(1, d.sp_n)]
        peers += [self.dev(self.zpeer(k), self.y) for k in range(1, d.z_n)]
        peers += [self.dev(self.z, self.ypeer(k)) for k in range(1, d.y_n)]
        for peer in peers:
            pl.semaphore_signal(sem, inc=1, device_id=peer, device_id_type=MESH)
        goal, source, stays = self.moved()

        @pl.when(jnp.logical_not(stays))
        def _():
            pl.semaphore_signal(sem, inc=1, device_id=goal, device_id_type=MESH)
            pl.semaphore_signal(sem, inc=1, device_id=source, device_id_type=MESH)
            pl.semaphore_wait(sem, len(peers) + 2)

        @pl.when(stays)
        def _():
            pl.semaphore_wait(sem, len(peers))


def rcopy(src, dst, send, recv, device):
    return pltpu.make_async_remote_copy(
        src_ref=src, dst_ref=dst, send_sem=send, recv_sem=recv, device_id=device, device_id_type=MESH
    )


class Gather:
    def __init__(self, p, send, recv):
        self.p, self.send, self.recv = p, send, recv

    def copy(self, buf, slot, way, device_slot):
        p = self.p
        return rcopy(
            buf.at[slot], buf.at[slot], self.send.at[way, device_slot], self.recv.at[slot], (p.r, device_slot)
        )

    def start(self, buf):
        p = self.p
        for dx in range(1, p.d.x_n):
            self.copy(buf, p.s, 0, p.slot(2 * dx)).start()
        self.copy(buf, p.s, 0, p.partner).start()

    def forward(self, buf, slot):
        p = self.p
        return rcopy(
            buf.at[slot], buf.at[slot], self.send.at[1, slot], self.recv.at[slot], (p.r, p.partner)
        )

    def take(self, buf, step):
        p = self.p
        slot = p.slot(step)

        @pl.when(step > 0)
        def _():
            rcopy(
                buf.at[slot], buf.at[slot], self.send.at[0, slot], self.recv.at[slot], (p.r, p.partner)
            ).wait_recv()

        @pl.when((step > 0) & (step % 2 == 0))
        def _():
            self.forward(buf, slot).start()

        return slot

    def end(self, buf):
        p = self.p
        for dx in range(1, p.d.x_n):
            self.copy(buf, p.s, 0, p.slot(2 * dx)).wait_send()
            self.forward(buf, p.slot(2 * dx)).wait_send()
        self.copy(buf, p.s, 0, p.partner).wait_send()


class Scatter:
    def __init__(self, p, part, near, far, near_send, near_recv, far_send, far_recv):
        self.p, self.part, self.near, self.far = p, part, near, far
        self.near_send, self.near_recv, self.far_send, self.far_recv = near_send, near_recv, far_send, far_recv

    def near_copy(self, x):
        p = self.p
        return rcopy(
            self.part.at[x * 2 + (p.c + 1) % 2],
            self.near.at[x],
            self.near_send.at[x],
            self.near_recv.at[x],
            (p.r, p.partner),
        )

    def far_copy(self, x, source):
        p = self.p
        return rcopy(
            self.part.at[x * 2 + p.c], self.far.at[source], self.far_send.at[x], self.far_recv.at[source], (p.r, x * 2 + p.c)
        )

    def put(self, step):
        p = self.p

        @pl.when(step % 2 == 1)
        def _():
            self.near_copy(p.slot(step) // 2).start()

    def cross(self):
        p = self.p
        for dx in range(1, p.d.x_n):
            x = (p.x + dx) % p.d.x_n
            self.near_copy(x).wait_recv()
            slot = x * 2 + p.c

            @pl.loop(0, p.d.tok // 64)
            def _(i):
                rows = pl.ds(pl.multiple_of(i * 64, 64), 64)
                both = self.part[slot, rows].astype(F32) + self.near[x, rows].astype(F32)
                self.part[slot, rows] = both.astype(BF)

            self.far_copy(x, p.x).start()

    def arrive(self):
        p = self.p
        self.near_copy(p.x).wait_recv()
        for dx in range(1, p.d.x_n):
            x = (p.x + dx) % p.d.x_n
            self.far_copy(x, x).wait_recv()

    def total(self, rows):
        p = self.p
        value = self.part[p.s, rows].astype(F32) + self.near[p.x, rows].astype(F32)
        for dx in range(1, p.d.x_n):
            value = value + self.far[(p.x + dx) % p.d.x_n, rows].astype(F32)
        return value

    def end(self):
        p = self.p
        for dx in range(p.d.x_n):
            x = (p.x + dx) % p.d.x_n
            self.near_copy(x).wait_send()
            if dx:
                self.far_copy(x, p.x).wait_send()


class SmallSum:
    def __init__(self, p, first, sp_in, mid_a, z_in, mid_b, y_in, sp_sem, z_sem, y_sem):
        self.p = p
        self.bufs = ((first, sp_in, sp_sem), (mid_a, z_in, z_sem), (mid_b, y_in, y_sem))

    def plan(self, stage):
        p = self.p
        if stage == 0:
            return p.s, [(p.slot(t), (p.r, p.slot(t))) for t in range(1, p.d.sp_n)]
        if stage == 1:
            return p.z, [(p.zpeer(k), p.dev(p.zpeer(k), p.y)) for k in range(1, p.d.z_n)]
        return p.y, [(p.ypeer(k), p.dev(p.z, p.ypeer(k))) for k in range(1, p.d.y_n)]

    def start(self, stage):
        src, dst, sem = self.bufs[stage]
        own, peers = self.plan(stage)
        for index, device in peers:
            rcopy(src, dst.at[own], sem.at[0, index], sem.at[1, own], device).start()

    def finish(self, stage, result):
        src, dst, sem = self.bufs[stage]
        own, peers = self.plan(stage)
        value = src[...]
        for index, device in peers:
            rcopy(src, dst.at[index], sem.at[0, index], sem.at[1, index], device).wait_recv()
            value = value + dst[index]
        result[...] = value
        for index, device in peers:
            rcopy(src, dst.at[own], sem.at[0, index], sem.at[1, own], device).wait_send()


def small_scratch(d):
    return [
        ("sp_in", pltpu.VMEM((d.sp_n, 8, d.width), F32)),
        ("mid_a", pltpu.VMEM((8, d.width), F32)),
        ("z_in", pltpu.VMEM((d.z_n, 8, d.width), F32)),
        ("mid_b", pltpu.VMEM((8, d.width), F32)),
        ("y_in", pltpu.VMEM((d.y_n, 8, d.width), F32)),
        ("sp_sem", pltpu.SemaphoreType.DMA((2, d.sp_n))),
        ("z_sem", pltpu.SemaphoreType.DMA((2, d.z_n))),
        ("y_sem", pltpu.SemaphoreType.DMA((2, d.y_n))),
    ]


def comm_scratch(d):
    return [
        ("part", pltpu.VMEM((d.sp_n, d.tok, d.width), BF)),
        ("near", pltpu.VMEM((d.x_n, d.tok, d.width), BF)),
        ("far", pltpu.VMEM((d.x_n, d.tok, d.width), BF)),
        ("ag_send", pltpu.SemaphoreType.DMA((2, d.sp_n))),
        ("ag_recv", pltpu.SemaphoreType.DMA((d.sp_n,))),
        ("near_send", pltpu.SemaphoreType.DMA((d.x_n,))),
        ("near_recv", pltpu.SemaphoreType.DMA((d.x_n,))),
        ("far_send", pltpu.SemaphoreType.DMA((d.x_n,))),
        ("far_recv", pltpu.SemaphoreType.DMA((d.x_n,))),
    ]


SAVED = ("xin", "qkv", "att", "probs", "xmid", "hid", "slope", "stream", "mid")
ONCE = ("qkv", "att", "probs", "hid", "slope")
WEIGHTS = ("wqkv", "wout", "wup", "wdown")


def saved_shapes(d):
    full = (d.sp_n, d.tok, d.width)
    return {
        "xin": (full, BF),
        "qkv": ((d.sp_n, d.tok, 3 * d.dh), BF),
        "att": ((d.sp_n, d.tok, d.dh), BF),
        "probs": ((d.heads, len(d.pairs), d.tok, d.tok), BF),
        "xmid": (full, BF),
        "hid": ((d.sp_n, d.tok, d.hid), BF),
        "slope": ((d.sp_n, d.tok, d.hid), BF),
        "stream": ((d.tok, d.width), F32),
        "mid": ((d.tok, d.width), F32),
    }


def weight_shapes(d):
    return {name: ((d.z_n, d.y_n) + d.block_shape(i), BF) for i, name in enumerate(WEIGHTS)}


class Fetch:
    def __init__(self, p, o):
        self.p, self.o = p, o
        self.full = (o.wqkv, o.wout, o.wup, o.wdown)

    def spread(self, l, w):
        p, o = self.p, self.o
        own = self.full[w].at[l, p.z, p.y]
        if w in (QKV, UP):
            src = o.in_qkv if w == QKV else o.in_up
            for t in range(1, p.d.sp_n):
                j = p.slot(t)
                rcopy(src.at[l, j], own.at[p.s], o.s_send.at[l, w, j], o.s_recv.at[l, w, p.s], (p.r, j)).start()
            pltpu.make_async_copy(src.at[l, p.s], own.at[p.s], o.own_sem.at[l, w]).start()
        elif w == DOWN:
            pltpu.make_async_copy(o.in_down.at[l], own, o.own_sem.at[l, w]).start()
        else:
            goal, _, stays = p.moved()

            @pl.when(stays)
            def _():
                pltpu.make_async_copy(o.in_out.at[l], own, o.own_sem.at[l, w]).start()

            @pl.when(jnp.logical_not(stays))
            def _():
                there = self.full[w].at[l, goal[0] // p.d.y_n, goal[0] % p.d.y_n]
                rcopy(o.in_out.at[l], there, o.s_send.at[l, w, 0], o.s_recv.at[l, w, 0], goal).start()

    def lines(self, l, w):
        p, o = self.p, self.o
        own = self.full[w].at[l, p.z, p.y]
        if w in (QKV, UP):
            src = o.in_qkv if w == QKV else o.in_up
            pltpu.make_async_copy(src.at[l, p.s], own.at[p.s], o.own_sem.at[l, w]).wait()
            for t in range(1, p.d.sp_n):
                j = p.slot(t)
                rcopy(src.at[l, j], own.at[j], o.s_send.at[l, w, j], o.s_recv.at[l, w, j], (p.r, j)).wait_recv()
        elif w == DOWN:
            pltpu.make_async_copy(o.in_down.at[l], own, o.own_sem.at[l, w]).wait()
        else:
            goal, _, stays = p.moved()

            @pl.when(stays)
            def _():
                pltpu.make_async_copy(o.in_out.at[l], own, o.own_sem.at[l, w]).wait()

            @pl.when(jnp.logical_not(stays))
            def _():
                rcopy(o.in_out.at[l], own, o.s_send.at[l, w, 0], o.s_recv.at[l, w, 0], goal).wait_recv()

        for k in range(1, p.d.z_n):
            self.z_copy(l, w, p.z, k).start()
        for k in range(1, p.d.y_n):
            self.y_copy(l, w, p.z, p.y, k).start()

    def z_copy(self, l, w, z, k):
        p, o = self.p, self.o
        block = self.full[w].at[l, z, p.y]
        there = p.zpeer(k)
        return rcopy(block, block, o.z_send.at[l, w, there], o.z_recv.at[l, w, z], p.dev(there, p.y))

    def y_copy(self, l, w, z, y, k):
        p, o = self.p, self.o
        block = self.full[w].at[l, z, y]
        there = p.ypeer(k)
        return rcopy(block, block, o.y_send.at[l, w, z, there], o.y_recv.at[l, w, z, y], p.dev(p.z, there))

    def onward(self, l, w):
        p = self.p
        for k in range(1, p.d.z_n):
            z = p.zpeer(k)
            self.z_copy(l, w, z, k).wait_recv()
            for m in range(1, p.d.y_n):
                self.y_copy(l, w, z, p.y, m).start()

    def ready(self, l, w):
        p, o = self.p, self.o
        for m in range(1, p.d.y_n):
            for k in range(p.d.z_n):
                self.y_copy(l, w, p.zpeer(k), p.ypeer(m), m).wait_recv()
        pltpu.make_async_copy(self.full[w].at[l], o.w_save[w].at[l], o.w_sem.at[l, w]).start()

    def end(self):
        p, o = self.p, self.o
        for l in range(p.d.layers):
            for w in range(4):
                own = self.full[w].at[l, p.z, p.y]
                if w in (QKV, UP):
                    src = o.in_qkv if w == QKV else o.in_up
                    for t in range(1, p.d.sp_n):
                        j = p.slot(t)
                        rcopy(src.at[l, j], own.at[p.s], o.s_send.at[l, w, j], o.s_recv.at[l, w, p.s], (p.r, j)).wait_send()
                elif w == OUT:
                    goal, _, stays = p.moved()

                    @pl.when(jnp.logical_not(stays))
                    def _():
                        rcopy(o.in_out.at[l], own, o.s_send.at[l, w, 0], o.s_recv.at[l, w, 0], goal).wait_send()

                for k in range(1, p.d.z_n):
                    self.z_copy(l, w, p.z, k).wait_send()
                for k in range(p.d.z_n):
                    for m in range(1, p.d.y_n):
                        self.y_copy(l, w, p.zpeer(k), p.y, m).wait_send()
                pltpu.make_async_copy(self.full[w].at[l], o.w_save[w].at[l], o.w_sem.at[l, w]).wait()


class Refs:
    pass


def mean_of(v):
    return jnp.mean(v, axis=-1, keepdims=True)


def norm_rows(v, gain):
    center = v - mean_of(v)
    return center * lax.rsqrt(mean_of(center * center) + EPS) * gain


def row_loop(tok, body, step=32):
    @pl.loop(0, tok // step)
    def _(i):
        body(pl.ds(pl.multiple_of(i * step, step), step))


def attention_forward(d, o, l):
    tok = d.tok
    for i in range(d.sp_n):
        here = o.meta[0, i]
        pos = i * tok + lax.broadcasted_iota(jnp.int32, (tok, 1), 0)
        start = jnp.zeros((tok, 1), jnp.int32)
        for b in range(1, d.docs):
            start = jnp.where(pos >= o.meta[2, b], o.meta[2, b], start)
        blocks = range(max(0, i - d.back), i + 1)
        for h in range(d.heads):
            lanes = slice(h * HD, (h + 1) * HD)
            query = o.qkv[0, here, :, lanes]
            scores = []
            for b in blocks:
                keys = o.qkv[0, o.meta[0, b], :, d.dh + h * HD : d.dh + (h + 1) * HD]
                key_pos = b * tok + lax.broadcasted_iota(jnp.int32, (tok, tok), 1)
                query_pos = i * tok + lax.broadcasted_iota(jnp.int32, (tok, tok), 0)
                score = nt(query, keys) * HD ** (-0.5) + o.head_slope[h] * (key_pos - query_pos).astype(F32)
                allowed = key_pos >= start
                if b == i:
                    allowed = allowed & (key_pos <= query_pos)
                scores.append(jnp.where(allowed, score, MASKED))
            top = scores[0].max(axis=-1, keepdims=True)
            for score in scores[1:]:
                top = jnp.maximum(top, score.max(axis=-1, keepdims=True))
            expo = [jnp.exp(score - top) for score in scores]
            total = expo[0].sum(axis=-1, keepdims=True)
            for part in expo[1:]:
                total = total + part.sum(axis=-1, keepdims=True)
            inverse = 1.0 / total
            result = None
            for b, part in zip(blocks, expo):
                low = (part * inverse).astype(BF)
                o.probs[0, h, d.pairs.index((i, b))] = low
                values = o.qkv[0, o.meta[0, b], :, 2 * d.dh + h * HD : 2 * d.dh + (h + 1) * HD]
                term = nn(low, values)
                result = term if result is None else result + term
            o.sorted_att[i, :, lanes] = result.astype(BF)


def fwd_kernel(d, names, *refs):
    o = Refs()
    for name, ref in zip(names, refs):
        setattr(o, name, ref)
    o.w_save = (o.o_wqkv, o.o_wout, o.o_wup, o.o_wdown)
    p = Place(d)
    p.barrier()
    fetch = Fetch(p, o)
    gather = Gather(p, o.ag_send, o.ag_recv)
    scatter = Scatter(p, o.part, o.near, o.far, o.near_send, o.near_recv, o.far_send, o.far_recv)
    small = SmallSum(p, o.in_gains, o.sp_in, o.mid_a, o.z_in, o.mid_b, o.y_in, o.sp_sem, o.z_sem, o.y_sem)

    def save(name, l):
        ref, out = getattr(o, name), getattr(o, "o_" + name)
        held = 0 if name in ONCE else l
        return pltpu.make_async_copy(ref.at[held], out.at[l], o.save_sem.at[l, SAVED.index(name)])

    def free(l, *names):
        if l > 0:
            for name in names:
                save(name, l - 1).wait()

    small.start(0)
    for w in range(4):
        fetch.spread(0, w)
    fetch.lines(0, QKV)
    small.finish(0, o.mid_a)
    small.start(1)
    fetch.lines(0, OUT)
    fetch.lines(0, UP)
    fetch.lines(0, DOWN)
    small.finish(1, o.mid_b)
    small.start(2)
    small.finish(2, o.o_gains)

    for l in range(d.layers):
        gain_in = o.o_gains[2 * l : 2 * l + 1, :]
        gain_mid = o.o_gains[2 * l + 1 : 2 * l + 2, :]

        if l == 0:

            def first(rows):
                v = o.in_tokens[rows, :].astype(F32)
                o.stream[0, rows] = v
                o.xin[0, p.s, rows] = norm_rows(v, gain_in).astype(BF)

            row_loop(d.tok, first)
        xin = o.xin.at[l]
        gather.start(xin)
        save("stream", l).start()
        if l == 0:
            fetch.onward(0, QKV)
            for later in range(1, d.layers):
                for w in range(4):
                    fetch.spread(later, w)
        else:
            fetch.onward(l, UP)
        fetch.ready(l, QKV)
        free(l, "qkv")

        @pl.loop(0, d.sp_n)
        def _(t):
            slot = gather.take(xin, t)
            block = xin[slot]
            for n in range(3 * d.dh // d.chunk if d.dh % d.chunk == 0 else 3):
                size = 3 * d.dh // (3 * d.dh // d.chunk if d.dh % d.chunk == 0 else 3)
                cols = slice(n * size, (n + 1) * size)
                weight = o.wqkv[l, :, :, :, :, cols].reshape(d.width, size)
                o.qkv[0, slot, :, cols] = nn(block, weight).astype(BF)

        gather.end(xin)
        save("xin", l).start()
        save("qkv", l).start()
        if l == 0:
            fetch.onward(0, OUT)
        free(l, "probs", "att")
        attention_forward(d, o, l)
        save("probs", l).start()
        fetch.onward(l, UP if l == 0 else DOWN)
        fetch.ready(l, OUT)

        @pl.loop(0, d.sp_n)
        def _(t):
            slot = p.slot(t)
            block = o.sorted_att[o.meta[1, slot]]
            o.att[0, slot] = block
            for n in range(d.n_width):
                cols = slice(n * d.chunk, (n + 1) * d.chunk)
                weight = o.wout[l, :, :, :, cols].reshape(d.dh, d.chunk)
                o.part[slot, :, cols] = nn(block, weight).astype(BF)
            scatter.put(t)

        save("att", l).start()
        scatter.cross()
        if l + 1 < d.layers:
            for w in range(4):
                fetch.lines(l + 1, w)
        scatter.arrive()
        xmid = o.xmid.at[l]

        def middle(rows):
            v = o.stream[l, rows] + scatter.total(rows)
            o.mid[l, rows] = v
            xmid[p.s, rows] = norm_rows(v, gain_mid).astype(BF)

        row_loop(d.tok, middle)
        scatter.end()
        gather.start(xmid)
        save("mid", l).start()
        if l == 0:
            fetch.onward(0, DOWN)
        fetch.ready(l, UP)
        fetch.ready(l, DOWN)
        free(l, "hid", "slope")

        @pl.loop(0, d.sp_n)
        def _(t):
            slot = gather.take(xmid, t)
            block = xmid[slot]
            for n in range(d.n_hid):
                cols = slice(n * d.chunk, (n + 1) * d.chunk)
                weight = o.wup[l, :, :, :, :, cols].reshape(d.width, d.chunk)
                pre = nn(block, weight)
                phi = 0.5 * (1.0 + lax.erf(pre * (0.5**0.5)))
                o.hid[0, slot, :, cols] = (pre * phi).astype(BF)
                density = jnp.exp(-0.5 * pre * pre) * 0.3989422804014327
                o.slope[0, slot, :, cols] = (phi + pre * density).astype(BF)
            hidden = o.hid[0, slot]
            for n in range(d.n_width):
                cols = slice(n * d.chunk, (n + 1) * d.chunk)
                weight = o.wdown[l, :, :, :, cols].reshape(d.hid, d.chunk)
                o.part[slot, :, cols] = nn(hidden, weight).astype(BF)
            scatter.put(t)

        gather.end(xmid)
        save("xmid", l).start()
        save("hid", l).start()
        save("slope", l).start()
        scatter.cross()
        if l + 1 < d.layers:
            fetch.onward(l + 1, QKV)
            fetch.onward(l + 1, OUT)
        scatter.arrive()
        if l + 1 < d.layers:
            gain_next = o.o_gains[2 * l + 2 : 2 * l + 3, :]

            def last(rows):
                v = o.mid[l, rows] + scatter.total(rows)
                o.stream[l + 1, rows] = v
                o.xin[l + 1, p.s, rows] = norm_rows(v, gain_next).astype(BF)

        else:

            def last(rows):
                o.o_output[rows, :] = (o.mid[l, rows] + scatter.total(rows)).astype(BF)

        row_loop(d.tok, last)
        scatter.end()

    fetch.end()
    for l in range(d.layers):
        for name in SAVED:
            if l == d.layers - 1 or name not in ONCE:
                save(name, l).wait()


class Reduce:
    def __init__(self, p, o):
        self.p, self.o = p, o
        self.grad = (o.g_qkv, o.g_out, o.g_up, o.g_down)
        self.y_in = (o.y_qkv, o.y_out, o.y_up, o.y_down)
        self.z_in = (o.z_qkv, o.z_out, o.z_up, o.z_down)
        self.sp_in = (o.x_qkv, o.x_out, o.x_up, None)
        self.result = (o.o_qkv, o.o_out, o.o_up, o.o_down)

    def y_copy(self, l, w, k):
        p, o = self.p, self.o
        index = p.d.y_n - k - 1
        there = p.ypeer(k)
        return rcopy(
            self.grad[w].at[:, there], self.y_in[w].at[l, index], o.ry_send.at[l, w, k], o.ry_recv.at[l, w, index], p.dev(p.z, there)
        )

    def z_copy(self, l, w, k):
        p, o = self.p, self.o
        index = p.d.z_n - k - 1
        there = p.zpeer(k)
        return rcopy(
            self.grad[w].at[there, p.y], self.z_in[w].at[l, index], o.rz_send.at[l, w, k], o.rz_recv.at[l, w, index], p.dev(there, p.y)
        )

    def begin(self, l, w):
        for k in range(1, self.p.d.y_n):
            self.y_copy(l, w, k).start()

    def add_rows(self, w, body):
        shape = self.p.d.block_shape(w)
        if len(shape) == 3:
            for j in range(shape[0]):
                body((j,))
        else:
            rows = 32 if shape[0] % 32 == 0 else shape[0]
            for j in range(shape[0] // rows):
                body((slice(j * rows, (j + 1) * rows),))

    def across(self, l, w):
        p = self.p
        for k in range(1, p.d.y_n):
            self.y_copy(l, w, p.d.y_n - k).wait_recv()
        for k in range(1, p.d.z_n):
            z = p.zpeer(k)

            def add(index):
                value = self.grad[w][(z, p.y) + index].astype(F32)
                for m in range(p.d.y_n - 1):
                    value = value + self.y_in[w][(l, m, z) + index].astype(F32)
                self.grad[w][(z, p.y) + index] = value.astype(BF)

            self.add_rows(w, add)
            self.z_copy(l, w, k).start()

    def s_copy(self, l, w, j, source):
        p, o = self.p, self.o
        return rcopy(
            self.grad[w].at[p.z, p.y, j], self.sp_in[w].at[l, source], o.rs_send.at[l, w, j], o.rs_recv.at[l, w, source], (p.r, j)
        )

    def settle(self, l, w):
        p, o = self.p, self.o
        for k in range(1, p.d.z_n):
            self.z_copy(l, w, p.d.z_n - k).wait_recv()

        def add(index):
            value = self.grad[w][(p.z, p.y) + index].astype(F32)
            for m in range(p.d.y_n - 1):
                value = value + self.y_in[w][(l, m, p.z) + index].astype(F32)
            for m in range(p.d.z_n - 1):
                value = value + self.z_in[w][(l, m) + index].astype(F32)
            if w == DOWN:
                self.result[w][(l,) + index] = value
            else:
                self.grad[w][(p.z, p.y) + index] = value.astype(BF)

        self.add_rows(w, add)
        if w in (QKV, UP):
            for t in range(1, p.d.sp_n):
                self.s_copy(l, w, p.slot(t), p.s).start()
            self.result[w][l, p.s] = self.grad[w][p.z, p.y, p.s].astype(F32)
        elif w == OUT:
            _, source, stays = p.moved()

            @pl.when(stays)
            def _():
                self.result[w][l] = self.grad[w][p.z, p.y].astype(F32)

            @pl.when(jnp.logical_not(stays))
            def _():
                self.out_copy(l, source).start()

    def out_copy(self, l, device):
        p, o = self.p, self.o
        return rcopy(
            self.grad[OUT].at[p.z, p.y], self.sp_in[OUT].at[l], o.rs_send.at[l, OUT, 0], o.rs_recv.at[l, OUT, 0], device
        )

    def sent(self, l, w):
        p = self.p
        for k in range(1, p.d.y_n):
            self.y_copy(l, w, k).wait_send()
        for k in range(1, p.d.z_n):
            self.z_copy(l, w, k).wait_send()
        if w in (QKV, UP):
            for t in range(1, p.d.sp_n):
                self.s_copy(l, w, p.slot(t), p.s).wait_send()
        elif w == OUT:
            _, source, stays = p.moved()

            @pl.when(jnp.logical_not(stays))
            def _():
                self.out_copy(l, source).wait_send()

    def last(self, l, w):
        p = self.p
        if w in (QKV, UP):
            for t in range(1, p.d.sp_n):
                j = p.slot(t)
                self.s_copy(l, w, j, j).wait_recv()
                self.result[w][l, j] = self.sp_in[w][l, j].astype(F32)
        elif w == OUT:
            _, source, stays = p.moved()

            @pl.when(jnp.logical_not(stays))
            def _():
                self.out_copy(l, source).wait_recv()
                self.result[w][l] = self.sp_in[w][l].astype(F32)


def norm_back(v, d_out, gain):
    center = v - mean_of(v)
    inverse = lax.rsqrt(mean_of(center * center) + EPS)
    unit = center * inverse
    gain_term = jnp.sum(d_out * unit, axis=0, keepdims=True)
    e = d_out * gain
    back = (e - mean_of(e) - unit * mean_of(e * unit)) * inverse
    return back, gain_term


def attention_backward(d, o):
    tok = d.tok
    for i in range(d.sp_n):
        here = o.meta[0, i]
        blocks = range(max(0, i - d.back), i + 1)
        for h in range(d.heads):
            lanes = slice(h * HD, (h + 1) * HD)
            key_lanes = slice(d.dh + h * HD, d.dh + (h + 1) * HD)
            value_lanes = slice(2 * d.dh + h * HD, 2 * d.dh + (h + 1) * HD)
            query = o.qkv[here, :, lanes]
            grad = o.d_att[here, :, lanes]
            d_probs, inner = [], None
            for b in blocks:
                low = o.probs[h, d.pairs.index((i, b))].astype(F32)
                term = nt(grad, o.qkv[o.meta[0, b], :, value_lanes])
                d_probs.append(term)
                weighted = jnp.sum(low * term, axis=-1, keepdims=True)
                inner = weighted if inner is None else inner + weighted
            d_query = None
            for b, term in zip(blocks, d_probs):
                low = o.probs[h, d.pairs.index((i, b))]
                d_score = (low.astype(F32) * (term - inner)).astype(BF)
                step = nn(d_score, o.qkv[o.meta[0, b], :, key_lanes])
                d_query = step if d_query is None else d_query + step
                d_key, d_value = tn(d_score, query), tn(low, grad)
                if b == i:
                    o.d_keys[b, :, lanes] = d_key
                    o.d_values[b, :, lanes] = d_value
                else:
                    o.d_keys[b, :, lanes] += d_key
                    o.d_values[b, :, lanes] += d_value
            o.sorted_dqkv[i, :, lanes] = (d_query * HD ** (-0.5)).astype(BF)
    for b in range(d.sp_n):
        o.sorted_dqkv[b, :, d.dh : 2 * d.dh] = (o.d_keys[b] * HD ** (-0.5)).astype(BF)
        o.sorted_dqkv[b, :, 2 * d.dh :] = o.d_values[b].astype(BF)


def bwd_kernel(d, names, *refs):
    o = Refs()
    for name, ref in zip(names, refs):
        setattr(o, name, ref)
    p = Place(d)
    gather = Gather(p, o.ag_send, o.ag_recv)
    scatter = Scatter(p, o.part, o.near, o.far, o.near_send, o.near_recv, o.far_send, o.far_recv)
    small = SmallSum(p, o.gain_sum, o.sp_in, o.mid_a, o.z_in, o.mid_b, o.y_in, o.sp_sem, o.z_sem, o.y_sem)
    reduce = Reduce(p, o)
    loads = WEIGHTS + SAVED

    def load(name, l):
        return pltpu.make_async_copy(getattr(o, "i_" + name).at[l], getattr(o, name), o.load_sem.at[loads.index(name)])

    def refill(l, *which):
        if l > 0:
            for name in which:
                load(name, l - 1).start()

    top = d.layers - 1
    for name in ("wdown", "slope", "wup", "hid", "xmid", "mid", "wout", "qkv", "probs", "att", "wqkv", "xin", "stream"):
        load(name, top).start()
    p.barrier()
    o.gain_sum[...] = jnp.zeros_like(o.gain_sum)

    def begin(rows):
        v = o.in_cotangent[rows, :].astype(F32)
        o.o_grad[rows, :] = v
        o.gl[p.s, rows] = v.astype(BF)

    row_loop(d.tok, begin)
    gather.start(o.gl)
    tokens = d.sp_n * d.tok
    per_width = d.chunk // (d.sp_n * d.rows)
    per_hid = d.chunk // d.hid_own

    for l in reversed(range(d.layers)):
        gain_in = o.in_gains[2 * l : 2 * l + 1, :]
        gain_mid = o.in_gains[2 * l + 1 : 2 * l + 2, :]

        def hid_rows(n):
            step = per_hid
            first = n * step
            flat = [(k // d.y_n, k % d.y_n) for k in range(first, first + step)]
            return flat

        load("wdown", l).wait()
        load("slope", l).wait()
        load("wup", l).wait()

        @pl.loop(0, d.sp_n)
        def _(t):
            slot = gather.take(o.gl, t)
            block = o.gl[slot]
            wdown = o.wdown
            for n in range(d.n_hid):
                cols = slice(n * d.chunk, (n + 1) * d.chunk)
                zs = slice(n * d.z_n // d.n_hid, (n + 1) * d.z_n // d.n_hid)
                weight = wdown[zs].reshape(d.chunk, d.width)
                d_hidden = nt(block, weight)
                o.slope[slot, :, cols] = (d_hidden * o.slope[slot, :, cols].astype(F32)).astype(BF)
            d_pre = o.slope[slot]
            for n in range(d.n_width):
                cols = slice(n * d.chunk, (n + 1) * d.chunk)
                zs = slice(n * d.z_n // d.n_width, (n + 1) * d.z_n // d.n_width)
                weight = o.wup[zs].reshape(d.chunk, d.hid)
                o.part[slot, :, cols] = nt(d_pre, weight).astype(BF)
            scatter.put(t)

        gather.end(o.gl)
        refill(l, "wdown", "wup")
        scatter.cross()
        load("hid", l).wait()
        if l < top:
            reduce.sent(l + 1, DOWN)
        grad_low = o.gl[...].reshape(tokens, d.width)
        for n in range(d.n_hid):
            left = o.hid[:, :, n * d.chunk : (n + 1) * d.chunk].reshape(tokens, d.chunk)
            zs = slice(n * d.z_n // d.n_hid, (n + 1) * d.z_n // d.n_hid)
            value = tn(left, o.gl[...].reshape(tokens, d.width)).astype(BF)
            o.g_down[zs] = value.reshape((d.z_n // d.n_hid, d.y_n, d.hid_own, d.width))
        reduce.begin(l, DOWN)
        refill(l, "hid")
        load("mid", l).wait()
        scatter.arrive()

        def middle(rows):
            back, gain_term = norm_back(o.mid[rows, :], scatter.total(rows), gain_mid)
            o.gain_sum[2 * l + 1 : 2 * l + 2, :] += gain_term
            value = o.o_grad[rows, :] + back
            o.o_grad[rows, :] = value
            o.ml[p.s, rows] = value.astype(BF)

        row_loop(d.tok, middle)
        scatter.end()
        gather.start(o.ml)
        refill(l, "mid")
        load("xmid", l).wait()
        if l < top:
            reduce.sent(l + 1, UP)
        for n in range(d.n_width):
            left = o.xmid[:, :, n * d.chunk : (n + 1) * d.chunk].reshape(tokens, d.chunk)
            zs = slice(n * d.z_n // d.n_width, (n + 1) * d.z_n // d.n_width)
            value = tn(left, o.slope[...].reshape(tokens, d.hid)).astype(BF)
            o.g_up[zs] = value.reshape((d.z_n // d.n_width, d.y_n, d.sp_n, d.rows, d.hid))
        reduce.begin(l, UP)
        reduce.across(l, DOWN)
        refill(l, "xmid", "slope")
        load("wout", l).wait()

        @pl.loop(0, d.sp_n)
        def _(t):
            slot = gather.take(o.ml, t)
            weight = o.wout[...].reshape(d.dh, d.width)
            o.d_att[slot] = nt(o.ml[slot], weight).astype(BF)

        gather.end(o.ml)
        refill(l, "wout")
        load("qkv", l).wait()
        load("probs", l).wait()
        attention_backward(d, o)
        refill(l, "qkv", "probs")
        reduce.settle(l, DOWN)
        reduce.across(l, UP)
        load("wqkv", l).wait()

        @pl.loop(0, d.sp_n)
        def _(t):
            slot = p.slot(t)
            block = o.sorted_dqkv[o.meta[1, slot]]
            o.d_qkv[slot] = block
            for n in range(d.n_width):
                cols = slice(n * d.chunk, (n + 1) * d.chunk)
                zs = slice(n * d.z_n // d.n_width, (n + 1) * d.z_n // d.n_width)
                weight = o.wqkv[zs].reshape(d.chunk, 3 * d.dh)
                o.part[slot, :, cols] = nt(block, weight).astype(BF)
            scatter.put(t)

        scatter.cross()
        refill(l, "wqkv")
        load("att", l).wait()
        if l < top:
            reduce.sent(l + 1, OUT)
        value = tn(o.att[...].reshape(tokens, d.dh), o.ml[...].reshape(tokens, d.width)).astype(BF)
        o.g_out[...] = value.reshape((d.z_n, d.y_n, d.rows, d.width))
        reduce.begin(l, OUT)
        refill(l, "att")
        load("xin", l).wait()
        if l < top:
            reduce.sent(l + 1, QKV)
        for n in range(d.n_width):
            left = o.xin[:, :, n * d.chunk : (n + 1) * d.chunk].reshape(tokens, d.chunk)
            zs = slice(n * d.z_n // d.n_width, (n + 1) * d.z_n // d.n_width)
            value = tn(left, o.d_qkv[...].reshape(tokens, 3 * d.dh)).astype(BF)
            o.g_qkv[zs] = value.reshape((d.z_n // d.n_width, d.y_n, d.sp_n, d.rows, 3 * d.dh))
        reduce.begin(l, QKV)
        refill(l, "xin")
        load("stream", l).wait()
        scatter.arrive()

        def lower(rows):
            back, gain_term = norm_back(o.stream[rows, :], scatter.total(rows), gain_in)
            o.gain_sum[2 * l : 2 * l + 1, :] += gain_term
            value = o.o_grad[rows, :] + back
            o.o_grad[rows, :] = value
            if l > 0:
                o.gl[p.s, rows] = value.astype(BF)

        row_loop(d.tok, lower)
        scatter.end()
        if l > 0:
            gather.start(o.gl)
        else:
            small.start(0)
        refill(l, "stream")
        reduce.settle(l, UP)
        reduce.across(l, OUT)
        reduce.across(l, QKV)
        if l == 0:
            small.finish(0, o.mid_a)
            small.start(1)
        reduce.settle(l, OUT)
        reduce.settle(l, QKV)

    small.finish(1, o.mid_b)
    small.start(2)
    small.finish(2, o.o_gains)
    for l in reversed(range(d.layers)):
        for w in (DOWN, UP, OUT, QKV):
            reduce.last(l, w)
    for w in (DOWN, UP, OUT, QKV):
        reduce.sent(0, w)


ANY = pl.BlockSpec(memory_space=pl.ANY)
VM = pl.BlockSpec(memory_space=pltpu.VMEM)
SM = pl.BlockSpec(memory_space=pltpu.SMEM)


def call(kernel, d, inputs, outputs, scratch, identity):
    names = [i[0] for i in inputs] + [i[0] for i in outputs] + [i[0] for i in scratch]
    results = pl.pallas_call(
        functools.partial(kernel, d, names),
        out_shape=[jax.ShapeDtypeStruct(i[2], i[3]) for i in outputs],
        in_specs=[i[1] for i in inputs],
        out_specs=[i[1] for i in outputs],
        scratch_shapes=[i[1] for i in scratch],
        compiler_params=pltpu.CompilerParams(
            collective_id=identity, has_side_effects=True, vmem_limit_bytes=61 * 1024 * 1024
        ),
        name=kernel.__name__,
    )(*[i[2] for i in inputs])
    return dict(zip([i[0] for i in outputs], results))


def shards(dp_n, sp_n, tokens, cotangent, w_qkv, w_out, w_up, w_down, gains, piece_order, doc_lengths):
    _, tok, width = tokens.shape
    layers, _, rows, _ = w_qkv.shape
    ff = w_up.shape[-1]
    d = Dims(dp_n, sp_n, layers, tok, width, ff, doc_lengths.shape[1])
    r, s = lax.axis_index("dp"), lax.axis_index("sp")

    order = piece_order[0]
    ids = jnp.arange(sp_n, dtype=jnp.int32)
    inverse = jnp.sum(jnp.where(order[None, :] == ids[:, None], ids[None, :], 0), axis=1).astype(jnp.int32)
    starts = (jnp.cumsum(doc_lengths[0]) - doc_lengths[0]).astype(jnp.int32)
    meta = jnp.zeros((3, max(sp_n, d.docs)), jnp.int32)
    meta = meta.at[0, :sp_n].set(inverse).at[1, :sp_n].set(order).at[2, : d.docs].set(starts)
    head_ids = (s * d.heads + jnp.arange(d.heads, dtype=jnp.int32)).astype(F32)
    head_slope = jnp.exp2(-8.0 * (head_ids + 1.0) / HEADS)
    own = gains.shape[-1]
    padded = jnp.zeros((8, width), F32)
    padded = lax.dynamic_update_slice(
        padded, gains.reshape(2 * layers, own).astype(F32), (0, (r * sp_n + s) * own)
    )
    in_qkv = w_qkv.reshape(layers, 3, rows, sp_n, d.dh).transpose(0, 3, 2, 1, 4).reshape(layers, sp_n, rows, 3 * d.dh)
    in_up = (
        w_up.reshape(layers, rows, dp_n, sp_n, d.hid_own).transpose(0, 3, 1, 2, 4).reshape(layers, sp_n, rows, d.hid)
    )

    saved, weights = saved_shapes(d), weight_shapes(d)
    dma = pltpu.SemaphoreType.DMA
    fwd = call(
        fwd_kernel,
        d,
        [
            ("meta", SM, meta),
            ("head_slope", SM, head_slope),
            ("in_tokens", VM, tokens[0]),
            ("in_gains", VM, padded),
            ("in_qkv", ANY, in_qkv),
            ("in_out", ANY, w_out),
            ("in_up", ANY, in_up),
            ("in_down", ANY, w_down),
        ],
        [("o_output", VM, (tok, width), BF), ("o_gains", VM, (8, width), F32)]
        + [("o_" + n, ANY, (layers,) + weights[n][0], BF) for n in WEIGHTS]
        + [("o_" + n, ANY, (layers,) + saved[n][0], saved[n][1]) for n in SAVED],
        [(n, pltpu.VMEM((layers,) + weights[n][0], BF)) for n in WEIGHTS]
        + [(n, pltpu.VMEM((1 if n in ONCE else layers,) + saved[n][0], saved[n][1])) for n in SAVED]
        + [("sorted_att", pltpu.VMEM(saved["att"][0], BF))]
        + small_scratch(d)
        + comm_scratch(d)
        + [
            ("s_send", dma((layers, 4, sp_n))),
            ("s_recv", dma((layers, 4, sp_n))),
            ("own_sem", dma((layers, 4))),
            ("z_send", dma((layers, 4, d.z_n))),
            ("z_recv", dma((layers, 4, d.z_n))),
            ("y_send", dma((layers, 4, d.z_n, d.y_n))),
            ("y_recv", dma((layers, 4, d.z_n, d.y_n))),
            ("w_sem", dma((layers, 4))),
            ("save_sem", dma((layers, len(SAVED)))),
        ],
        0,
    )
    kinds = ("qkv", "out", "up", "down")
    blocks = [d.block_shape(w) for w in range(4)]
    bwd = call(
        bwd_kernel,
        d,
        [("meta", SM, meta), ("in_cotangent", VM, cotangent[0]), ("in_gains", VM, fwd["o_gains"])]
        + [("i_" + n, ANY, fwd["o_" + n]) for n in WEIGHTS + SAVED],
        [("o_grad", VM, (tok, width), F32), ("o_gains", VM, (8, width), F32)]
        + [("o_" + k, VM, (layers,) + b, F32) for k, b in zip(kinds, blocks)],
        [(n, pltpu.VMEM(weights[n][0], BF)) for n in WEIGHTS]
        + [(n, pltpu.VMEM(saved[n][0], saved[n][1])) for n in SAVED]
        + [
            ("gl", pltpu.VMEM((sp_n, tok, width), BF)),
            ("ml", pltpu.VMEM((sp_n, tok, width), BF)),
            ("d_att", pltpu.VMEM((sp_n, tok, d.dh), BF)),
            ("sorted_dqkv", pltpu.VMEM((sp_n, tok, 3 * d.dh), BF)),
            ("d_qkv", pltpu.VMEM((sp_n, tok, 3 * d.dh), BF)),
            ("d_keys", pltpu.VMEM((sp_n, tok, d.dh), F32)),
            ("d_values", pltpu.VMEM((sp_n, tok, d.dh), F32)),
            ("gain_sum", pltpu.VMEM((8, width), F32)),
        ]
        + [("g_" + k, pltpu.VMEM((d.z_n, d.y_n) + b, BF)) for k, b in zip(kinds, blocks)]
        + [("y_" + k, pltpu.VMEM((layers, max(1, d.y_n - 1), d.z_n) + b, BF)) for k, b in zip(kinds, blocks)]
        + [("z_" + k, pltpu.VMEM((layers, max(1, d.z_n - 1)) + b, BF)) for k, b in zip(kinds, blocks)]
        + [("x_" + k, pltpu.VMEM((layers,) + b, BF)) for k, b in zip(kinds[:3], blocks)]
        + small_scratch(d)
        + comm_scratch(d)
        + [
            ("load_sem", dma((len(WEIGHTS + SAVED),))),
            ("ry_send", dma((layers, 4, d.y_n))),
            ("ry_recv", dma((layers, 4, d.y_n))),
            ("rz_send", dma((layers, 4, d.z_n))),
            ("rz_recv", dma((layers, 4, d.z_n))),
            ("rs_send", dma((layers, 4, sp_n))),
            ("rs_recv", dma((layers, 4, sp_n))),
        ],
        1,
    )
    grad_qkv = bwd["o_qkv"].reshape(layers, sp_n, rows, 3, d.dh).transpose(0, 3, 2, 1, 4).reshape(w_qkv.shape)
    grad_up = (
        bwd["o_up"].reshape(layers, sp_n, rows, dp_n, d.hid_own).transpose(0, 2, 3, 1, 4).reshape(w_up.shape)
    )
    grad_gains = lax.dynamic_slice(bwd["o_gains"], (0, (r * sp_n + s) * own), (2 * layers, own))
    return (
        fwd["o_output"][None],
        bwd["o_grad"][None],
        grad_qkv,
        bwd["o_out"],
        grad_up,
        bwd["o_down"],
        grad_gains.reshape(gains.shape),
    )


def solution(mesh):
    return jax.shard_map(
        functools.partial(shards, mesh.shape["dp"], mesh.shape["sp"]),
        mesh=mesh,
        in_specs=(
            P("dp", "sp", None),
            P("dp", "sp", None),
            P(None, None, ("dp", "sp"), None),
            P(None, ("dp", "sp"), None),
            P(None, ("dp", "sp"), None),
            P(None, ("dp", "sp"), None),
            P(None, None, ("dp", "sp")),
            P("dp", None),
            P("dp", None),
        ),
        out_specs=(
            P("dp", "sp", None),
            P("dp", "sp", None),
            P(None, None, ("dp", "sp"), None),
            P(None, ("dp", "sp"), None),
            P(None, ("dp", "sp"), None),
            P(None, ("dp", "sp"), None),
            P(None, None, ("dp", "sp")),
        ),
        check_vma=False,
    )
```

time: 2590 us -> 486 us (0.19)
  waiting for transfers between devices: 1950 us -> 0 us
  Pallas kernels: 0 us -> 456 us
  matrix products: 266 us -> 0 us
  local copies, waits for them, and re-layouts: 143 us -> 19.2 us
  blocking collectives: 65.7 us -> 0 us
  starting transfers between devices: 56.3 us -> 0 us
  other arithmetic: 51.8 us -> 3.46 us
    reduce_scatter x6 -> x0, waiting for transfers between devices: 1020 us -> none  [the longest x2 371 us: shards(): lax.psum_scatter(terms[2], ('dp', 'sp'), scatter_dimension=0, tiled=True)]
    unnamed x20 -> x0, waiting for transfers between devices: 553 us -> none
    pallas_call x0 -> x2, Pallas kernels: none -> 456 us  [call(): pl.pallas_call(functools.partial(kernel, d, names), out_shape=[jax.ShapeD...]
    all_gather x8 -> x0, waiting for transfers between devices: 300 us -> none  [the longest x2 151 us: fetch(): lax.all_gather(w_down[layer_id], ('dp', 'sp'), axis=0, tiled=True)]
    dot_general x58 -> x0, matrix products: 244 us -> none  [the longest x2 39.6 us: layer_forward(): result = mid + jnp.dot(hidden, w_down, preferred_element_type=jnp.float32)]
    all_to_all x10 -> x0, waiting for transfers between devices: 82.7 us -> none  [the longest x2 40.2 us: layer_forward(): lax.all_to_all(projected, 'sp', split_axis=3, concat_axis=2, tiled=True)]
    all_gather x2 -> x0, blocking collectives: 65.7 us -> none  [fetch(): lax.all_gather(gains[layer_id], ('dp', 'sp'), axis=1, tiled=True)]
    all_to_all x10 -> x0, starting transfers between devices: 54.8 us -> none  [the longest x4 20.9 us: layer_forward(): lax.all_to_all(attended, 'sp', split_axis=1, concat_axis=2, tiled=True)]
  transfers between devices with their start and end apart: 27 -> 0, of which waited for: 20 -> 0; matrix products, arithmetic and copies ran while one was open for 14% -> 0% of each run, Pallas kernels for 0% -> 0%
where the time goes in v1:
time: 486 us; the launch traced here: 480 us
  Pallas kernels  456 us (94%)
  local copies, waits for them, and re-layouts  19.2 us (4%)
    pallas_call x2, Pallas kernels, call(): pl.pallas_call(functools.partial(kernel, d, names), out_shape=[jax.ShapeD...  456 us

profile of v1, /device:TPU:14, one launch (start us, length us, event | category | flops | bytes accessed | tf_op | source)
XLA Modules:
  0.0 479.8 jit_solution(17753296854427794173)
XLA Ops:
  0.6 0.5 multiply_exponential_fusion.refs_1_
  1.2 0.8 select_reduce_fusion
  1.9 0.8 reduce-window_1_clone.1
  2.8 0.7 sub.4
  3.4 0.7 scatter.11
  4.1 0.0 copy-start.4
  4.1 0.7 convert.1
  4.8 0.5 dynamic_update_slice.3.refs_3_
  5.3 0.0 copy-start.3
  5.3 1.3 reshape.128
  6.6 0.3 copy.35
  7.0 1.2 reshape.129.refs_4_
  8.2 1.4 reshape.130
  9.6 0.1 copy.34
  9.6 1.0 reshape.131.refs_6_
  10.7 0.0 copy-done.4
  10.7 0.0 copy-done.3
  10.7 220.1 %fwd_kernel.1 = (bf16[256,1024]{1,0:T(8,128)(2,1)}, f32[8,1024]{1,0:T(8,128)}, bf16[2,4,2,4,32,768]{5,4,3,2,1,0:T(8,128)(2,1)}, bf16[2,4,2,32,1024]{4,3,2,1,0:T(...) custom-call(s32[3,4]{1,0:T(4,128)} %copy-done.4, ...), custom_call_target="tpu_custom_call" | custom-call | tf_op jit(solution)/shard_map/fwd_kernel/pallas_call | solution.py:1021
  230.8 236.0 %bwd_kernel.1 = (f32[256,1024]{1,0:T(8,128)}, f32[8,1024]{1,0:T(8,128)}, f32[2,4,32,768]{3,2,1,0:T(8,128)}, f32[2,32,1024]{2,1,0:T(8,128)}, f32[2,4,32,1024]{3,2,1,0:T(8,128)}, /*index=5*/f32[2,128,1024]{2,1,0:T(8,128)}) custom-call(s32[3,4]{1,0:T(4,128)} %copy-done.4, bf16[256,1024]{1,0:T(8,128)(2,1)} %bitcast.35, f32[8,1024]{1,0:T(8,128)} %get-tuple-element.65.refs_2_, ...), custom_call_target="tpu_custom_call" | custom-call | tf_op jit(solution)/shard_map/bwd_kernel/pallas_call | solution.py:1021
  466.8 1.3 constant_dynamic-slice_fusion
  468.2 1.5 reshape.132
  469.7 0.5 copy.29
  470.2 0.0 copy-start.1
  470.2 1.3 reshape.133
  471.5 1.4 copy.31
  472.9 0.0 copy-start.2
  473.0 0.0 copy-start
  473.0 0.7 copy.30
  473.6 1.4 reshape.135
  475.0 1.9 copy.43
  476.9 0.0 copy-done.1
  476.9 1.0 copy.44
  477.9 0.0 copy-done.2
  477.9 0.7 copy.45
  478.6 0.0 copy-done
  478.6 1.0 copy.46
  (3 shorter events, 0.0 us)
Async XLA Ops:
  4.1 6.5 %copy-start.4 = (s32[3,4]{1,0:T(4,128)}, s32[3,4]{1,0:T(4,128)S(1)}, u32[]{:S(2)}) copy-start(s32[3,4]{1,0:T(4,128)S(1)} %scatter.14.refs_0_) | copy-start | bytes 148
  5.3 5.4 %copy-start.3 = (f32[8,1024]{1,0:T(8,128)}, f32[8,1024]{1,0:T(8,128)S(1)}, u32[]{:S(2)}) copy-start(f32[8,1024]{1,0:T(8,128)S(1)} %dynamic_update_slice.3.refs_3_) | copy-start | bytes 98308
  470.2 6.7 %copy-start.1 = (f32[256,1024]{1,0:T(8,128)S(1)}, f32[256,1024]{1,0:T(8,128)}, u32[]{:S(2)}) copy-start(f32[256,1024]{1,0:T(8,128)} %get-tuple-element.79) | copy-start | bytes 3145732
  472.9 4.9 %copy-start.2 = (f32[2,32,1024]{2,1,0:T(8,128)S(1)}, f32[2,32,1024]{2,1,0:T(8,128)}, u32[]{:S(2)}) copy-start(f32[2,32,1024]{2,1,0:T(8,128)} %get-tuple-element.95) | copy-start | bytes 786436
  473.0 5.6 %copy-start = (f32[2,128,1024]{2,1,0:T(8,128)S(1)}, f32[2,128,1024]{2,1,0:T(8,128)}, u32[]{:S(2)}) copy-start(f32[2,128,1024]{2,1,0:T(8,128)} %get-tuple-element.97) | copy-start | bytes 3145732
